TPU v7x, 32 devices: a whole 2x2x4 slice. The times are simulated.
32 devices in a mesh: segment: 2 (over x), row: 4 (over y, core), col: 4 (over z).
Axes of the slice: x: 2, y: 2, z: 4, core: 2. Of those that a mesh axis runs over, the one named last changes fastest.
Arguments:
- dosage: float32 [2048, 6144], P(('segment', 'col'), 'row'), may hold values from 0 to 2, as said below
- missing: int32 [2048, 6144], P(('segment', 'col'), 'row'), may hold values 0 or 1
- residuals: bfloat16 [6144, 256], P('row'), may hold values from -6 to 6
- global_grm: bfloat16 [6144, 6144], P('row', 'col'), may hold values from -1 to 2
- seg_counts: int32 [6], replicated, may hold values from 1 to 1024, 2048 in all
Outputs:
- scores: bfloat16 [6, 6144, 256], P(None, ('row', 'col'), 'segment')
Inputs may be any that keep to these rules, and one draw needn't show every extreme that they name: `dosage`: imputed alternative-allele dosages. 1 marks a missing genotype. `seg_counts`: SNP counts of the 6 segments, laid end to end over the 2048 variants; they sum to 2048 and the largest is exactly 1024.
All inputs are finite; a program needn't handle non-finite values. No bound on the sum of `missing` on one device may be relied on, other than what follows from the above.
Results may differ from a plain program's by a relative error of at most 0.0053.
Values may be sent and summed in bfloat16 or wider, within the bound.
No kernel may reach another device: no remote copies, remote signals or barrier semaphores. Data moves between devices by JAX's collectives and lax.ppermute only.
A program may use at most 320 MiB of HBM per device.

v0:
```python
import jax
import jax.numpy as jnp
from jax import lax
from jax.sharding import PartitionSpec as P

MOST = 1024
BLOCK = 256


def broadcast(shard, axis, root):
    mine = lax.axis_index(axis) == root
    return lax.psum(jnp.where(mine, shard, jnp.zeros_like(shard)), axis)


def gram_update(total, row_geno, col_geno, lower, upper, block_num):
    variants = row_geno.shape[0]
    nominal = lower + block_num * BLOCK
    first_row = jnp.minimum(nominal, variants - BLOCK)
    left_block = lax.dynamic_slice_in_dim(row_geno, first_row, BLOCK, 0)
    right_block = lax.dynamic_slice_in_dim(col_geno, first_row, BLOCK, 0)
    var_index = first_row + jnp.arange(BLOCK, dtype=jnp.int32)
    keep_mask = (var_index >= nominal) & (var_index < upper)
    left_block = jnp.where(keep_mask[:, None], left_block, jnp.zeros_like(left_block))
    return total + lax.dot_general(
        left_block, right_block, (((0,), (0,)), ((), ())), preferred_element_type=jnp.float32
    )


def segment_gram(row_geno, col_geno, lower, upper):
    local_gram = jnp.zeros((row_geno.shape[1], col_geno.shape[1]), jnp.float32)
    for block_num in range(MOST // BLOCK):

        def with_block(carry, block_num=block_num):
            return gram_update(carry, row_geno, col_geno, lower, upper, block_num)

        def without_block(carry):
            return carry

        local_gram = lax.cond(
            upper - lower > block_num * BLOCK, with_block, without_block, local_gram
        )
    return local_gram


def make_hadamard(local_gram, seg_count, global_grm):
    return (local_gram / seg_count.astype(jnp.float32) * global_grm).astype(jnp.bfloat16)


def shards(dosage, missing, residuals, global_grm, seg_counts):
    observed = (1 - missing).astype(jnp.float32)
    alt_local = jnp.sum(dosage * observed, axis=1)
    obs_local = jnp.sum(observed, axis=1)
    alt_total, obs_total = lax.psum((alt_local, obs_local), "row")
    allele_freq = (alt_total + 1.0) / (2.0 * obs_total + 2.0)
    allele_spread = jnp.sqrt(2.0 * allele_freq * (1.0 - allele_freq))
    standard = (observed * (dosage - 2.0 * allele_freq[:, None]) / allele_spread[:, None]).astype(
        jnp.bfloat16
    )
    group_id = lax.axis_index("segment")
    group_count = lax.axis_size("segment")
    col_count = lax.axis_size("col")
    segments = seg_counts.shape[0]
    seg_starts = jnp.cumsum(seg_counts) - seg_counts
    tile_size = standard.shape[1]
    dev_rows = tile_size // col_count
    half_cols = residuals.shape[1] // group_count
    row_geno = lax.all_gather(standard, "col", axis=0, tiled=True)
    col_geno, col_res = (
        broadcast(row_geno, "row", lax.axis_index("col")),
        broadcast(residuals, "row", lax.axis_index("col")),
    )
    half_vars = row_geno.shape[0]
    lower_bound = group_id * half_vars
    hadamards = []
    for segment_num in range(segments):
        seg_count = seg_counts[segment_num]
        seg_start = seg_starts[segment_num]
        lower = jnp.clip(seg_start - lower_bound, 0, half_vars)
        upper = jnp.clip(seg_start + seg_count - lower_bound, 0, half_vars)
        hadamards.append(
            make_hadamard(segment_gram(row_geno, col_geno, lower, upper), seg_count, global_grm)
        )
    summed = lax.psum_scatter(
        jnp.concatenate(
            [
                jnp.dot(hadamard, col_res, preferred_element_type=jnp.float32)
                for hadamard in hadamards
            ],
            axis=1,
        ),
        "col",
        scatter_dimension=0,
        tiled=True,
    )
    shaped = summed.reshape(dev_rows, segments, group_count, half_cols)
    reduced = lax.psum_scatter(
        shaped.astype(jnp.bfloat16), "segment", scatter_dimension=2, tiled=True
    ).astype(jnp.float32)
    scores = reduced.reshape(dev_rows, segments, half_cols).transpose(1, 0, 2)
    return scores.astype(jnp.bfloat16)


def solution(mesh):
    placed = (
        P(("segment", "col"), "row"),
        P(("segment", "col"), "row"),
        P("row", None),
        P("row", "col"),
        P(),
    )
    return jax.shard_map(
        shards,
        mesh=mesh,
        in_specs=placed,
        out_specs=P(None, ("row", "col"), "segment"),
        check_vma=False,
    )
```

profile of v0, /device:TPU:0, one launch (start us, length us, event | category | flops | bytes accessed | tf_op | source)
XLA Modules:
  0.0 463.6 jit_solution(2223579467096411345)
XLA Ops:
  6.5 2.2 multiply_reduce_fusion
  8.8 8.4 %all-reduce = (f32[256]{0:T(256)S(1)}, f32[256]{0:T(256)S(1)}) all-reduce(f32[256]{0:T(256)S(1)} %get-tuple-element.438, f32[256]{0:T(256)S(1)} %get-tuple-element.437), channel_id=1, replica_groups=mesh['segment'=2,'row'=4,'col'=4] {'row'}, use_global_device_ids=true, to_apply=%region_4.0 | all-reduce | flops 512 | bytes 4096 | tf_op jit(solution)/shard_map/psum | solution.py:53
  17.2 3.2 divide_convert_fusion
  20.3 0.0 all-gather.2.cloned.1.call-update
  20.3 0.0 all-reduce.4.cloned.1.call-start
  20.4 2.1 broadcast_select_fusion.1
  22.5 61.8 %all-gather.2.cloned.1.call-done = bf16[1024,1536]{1,0:T(8,128)(2,1)} async-done(((bf16[256,1536]{1,0:T(8,128)(2,1)}), bf16[1024,1536]{1,0:T(8,128)(2,1)}) %all-gather.2.cloned.1.call-update) | async-done | bytes 3145744 | tf_op jit(solution)/shard_map/all_gather | solution.py:67
  84.3 4.0 broadcast_select_fusion
  88.2 0.0 all-reduce.4.cloned.1.call-update
  88.3 0.0 reduce-scatter.3.cloned.1.call-start
  88.3 0.0 copy-done.1
  88.3 0.7 fusion.210
  89.6 0.2 reduce-window.9
  89.8 0.7 fusion.211
  105.2 63.3 %all-reduce.4.cloned.1.call-done = (bf16[1536,256]{1,0:T(8,128)(2,1)}, bf16[1024,1536]{1,0:T(8,128)(2,1)}) async-done(((bf16[1536,256]{1,0:T(8,128)(2,1)}, bf16[1024,1536]{1,0:T(8,128)(2,1)}), (bf16[1536,256]{1,0:T(8,128)(2,1)}, bf16[1024,1536]{1,0:T(8,128)(2,1)})) %all-reduce.4.cloned.1.call-update) | async-done | bytes 3932176 | tf_op jit(solution)/shard_map/psum | solution.py:12
  168.5 6.3 %conditional.24 = (f32[1536,1536]{1,0:T(8,128)}) conditional(s32[]{:T(128)} %convert_element_type.139, () %tuple.149, (s32[]{:T(128)}, s32[]{:T(128)}, bf16[1024,1536]{1,0:T(8,128)(2,1)S(1)}, bf16[1024,1536]{1,0:T(8,128)(2,1)}) %tuple.248), branch_computations={%region_6.7_spmd, %region_7.8_spmd} | conditional | flops 1208353792 | bytes 11011906 | solution.py:39
  168.5 6.3 %fusion = f32[1536,1536]{1,0:T(8,128)} fusion(bf16[1024,1536]{1,0:T(8,128)(2,1)} %get-tuple-element.324, s32[]{:T(128)S(6)} %select_n.133, bf16[1024,1536]{1,0:T(8,128)(2,1)S(1)} %get-tuple-element.317, pred[256]{0:T(512)(128)(4,1)S(1)} %compare_and_fusion), kind=kOutput, calls=%fused_computation | convolution fusion | flops 1208352768 | bytes 11011584 | tf_op jit(solution)/shard_map/cond/branch_1_fun/dot_general | solution.py:24
  174.8 6.3 %conditional.28 = (f32[1536,1536]{1,0:T(8,128)}) conditional(s32[]{:T(128)} %convert_element_type.148, () %tuple.154, (s32[]{:T(128)}, s32[]{:T(128)}, bf16[1024,1536]{1,0:T(8,128)(2,1)S(1)}, bf16[1024,1536]{1,0:T(8,128)(2,1)}) %tuple.252), branch_computations={%region_15.16_spmd, %region_16.17_spmd} | conditional | flops 1208353792 | bytes 11011906 | solution.py:39
  174.8 6.3 %fusion.29 = f32[1536,1536]{1,0:T(8,128)} fusion(bf16[1024,1536]{1,0:T(8,128)(2,1)} %get-tuple-element.345, s32[]{:T(128)S(6)} %select_n.141, bf16[1024,1536]{1,0:T(8,128)(2,1)S(1)} %get-tuple-element.344, pred[256]{0:T(512)(128)(4,1)S(1)} %compare_and_fusion.4), kind=kOutput, calls=%fused_computation.36 | convolution fusion | flops 1208352768 | bytes 11011584 | tf_op jit(solution)/shard_map/cond/branch_1_fun/dot_general | solution.py:24
  181.1 9.6 %conditional.29 = (f32[1536,1536]{1,0:T(8,128)}) conditional(s32[]{:T(128)} %convert_element_type.147, f32[1536,1536]{1,0:T(8,128)} %get-tuple-element.463, (s32[]{:T(128)}, s32[]{:T(128)}, bf16[1024,1536]{1,0:T(8,128)(2,1)S(1)}, bf16[1024,1536]{1,0:T(8,128)(2,1)}, f32[1536,1536]{1,0:T(8,128)}) %tuple.253), branch_computations={%region_17.18_spmd, %region_18.19_spmd} | conditional | flops 1210713088 | bytes 20449102 | solution.py:39
  181.6 9.2 %convolution_add_fusion.3 = f32[1536,1536]{1,0:T(8,128)} fusion(f32[1536,1536]{1,0:T(8,128)} %get-tuple-element.346, bf16[1024,1536]{1,0:T(8,128)(2,1)} %get-tuple-element.350, s32[]{:T(128)S(6)} %select_n.143, bf16[1024,1536]{1,0:T(8,128)(2,1)S(1)} %get-tuple-element.349, pred[256]{0:T(512)(128)(4,1)S(1)} %compare_and_fusion.5), kind=kOutput, calls=%fused_computation.45 | convolution fusion | flops 1210712064 | bytes 20448768 | tf_op jit(solution)/shard_map/cond/branch_1_fun/dot_general | solution.py:24
  190.8 9.1 %conditional.30 = (f32[1536,1536]{1,0:T(8,128)}) conditional(s32[]{:T(128)} %convert_element_type.146, f32[1536,1536]{1,0:T(8,128)} %get-tuple-element.464, (s32[]{:T(128)}, s32[]{:T(128)}, bf16[1024,1536]{1,0:T(8,128)(2,1)S(1)}, bf16[1024,1536]{1,0:T(8,128)(2,1)}, f32[1536,1536]{1,0:T(8,128)}) %tuple.254), branch_computations={%region_19.20_spmd, %region_20.21_spmd} | conditional | flops 1210713088 | bytes 20449102 | solution.py:39
  190.8 9.1 %convolution_add_fusion.4 = f32[1536,1536]{1,0:T(8,128)} fusion(f32[1536,1536]{1,0:T(8,128)} %get-tuple-element.351, bf16[1024,1536]{1,0:T(8,128)(2,1)} %get-tuple-element.355, s32[]{:T(128)S(6)} %select_n.145, bf16[1024,1536]{1,0:T(8,128)(2,1)S(1)} %get-tuple-element.354, pred[256]{0:T(512)(128)(4,1)S(1)} %compare_and_fusion.6), kind=kOutput, calls=%fused_computation.54 | convolution fusion | flops 1210712064 | bytes 20448768 | tf_op jit(solution)/shard_map/cond/branch_1_fun/dot_general | solution.py:24
  199.9 9.1 %conditional.31 = (f32[1536,1536]{1,0:T(8,128)}) conditional(s32[]{:T(128)} %convert_element_type.145, f32[1536,1536]{1,0:T(8,128)} %get-tuple-element.465, (s32[]{:T(128)}, s32[]{:T(128)}, bf16[1024,1536]{1,0:T(8,128)(2,1)S(1)}, bf16[1024,1536]{1,0:T(8,128)(2,1)}, f32[1536,1536]{1,0:T(8,128)}) %tuple.255), branch_computations={%region_21.22_spmd, %region_22.23_spmd} | conditional | flops 1210713088 | bytes 20449102 | solution.py:39
  199.9 9.1 %convolution_add_fusion.5 = f32[1536,1536]{1,0:T(8,128)} fusion(f32[1536,1536]{1,0:T(8,128)} %get-tuple-element.356, bf16[1024,1536]{1,0:T(8,128)(2,1)} %get-tuple-element.360, s32[]{:T(128)S(6)} %select_n.147, bf16[1024,1536]{1,0:T(8,128)(2,1)S(1)} %get-tuple-element.359, pred[256]{0:T(512)(128)(4,1)S(1)} %compare_and_fusion.7), kind=kOutput, calls=%fused_computation.63 | convolution fusion | flops 1210712064 | bytes 20448768 | tf_op jit(solution)/shard_map/cond/branch_1_fun/dot_general | solution.py:24
  209.0 4.9 %conditional.32 = (f32[1536,1536]{1,0:T(8,128)}) conditional(s32[]{:T(128)} %convert_element_type.154, () %tuple.159, (s32[]{:T(128)}, s32[]{:T(128)}, bf16[1024,1536]{1,0:T(8,128)(2,1)S(1)}, bf16[1024,1536]{1,0:T(8,128)(2,1)}) %tuple.256), branch_computations={%region_23.24_spmd, %region_24.25_spmd} | conditional | flops 1208353792 | bytes 11011906 | solution.py:39
  209.0 4.9 %broadcast.365 = f32[1536,1536]{1,0:T(8,128)} broadcast(f32[]{:T(128)} %constant.12.clone), dimensions={} | broadcast | bytes 9437188 | tf_op jit(solution)/shard_map/broadcast.23
  213.9 0.2 conditional.35
  214.1 4.9 %conditional.36 = (f32[1536,1536]{1,0:T(8,128)}) conditional(s32[]{:T(128)} %convert_element_type.160, () %tuple.164, (s32[]{:T(128)}, s32[]{:T(128)}, bf16[1024,1536]{1,0:T(8,128)(2,1)S(1)}, bf16[1024,1536]{1,0:T(8,128)(2,1)}) %tuple.260), branch_computations={%region_31.32_spmd, %region_32.33_spmd} | conditional | flops 1208353792 | bytes 11011906 | solution.py:39
  214.1 4.9 %broadcast.370 = f32[1536,1536]{1,0:T(8,128)} broadcast(f32[]{:T(128)} %constant.16.clone), dimensions={} | broadcast | bytes 9437188 | tf_op jit(solution)/shard_map/broadcast.33
  218.9 4.7 %conditional.40 = (f32[1536,1536]{1,0:T(8,128)}) conditional(s32[]{:T(128)} %convert_element_type.166, () %tuple.169, (s32[]{:T(128)}, s32[]{:T(128)}, bf16[1024,1536]{1,0:T(8,128)(2,1)S(1)}, bf16[1024,1536]{1,0:T(8,128)(2,1)}) %tuple.264), branch_computations={%region_39.40_spmd, %region_40.41_spmd} | conditional | flops 1208353792 | bytes 11011906 | solution.py:39
  218.9 4.7 %broadcast.375 = f32[1536,1536]{1,0:T(8,128)} broadcast(f32[]{:T(128)} %constant.38.clone), dimensions={} | broadcast | bytes 9437188 | tf_op jit(solution)/shard_map/broadcast.43
  223.7 0.2 conditional.41
  223.9 4.7 %conditional.44 = (f32[1536,1536]{1,0:T(8,128)}) conditional(s32[]{:T(128)} %convert_element_type.172, () %tuple.174, (s32[]{:T(128)}, s32[]{:T(128)}, bf16[1024,1536]{1,0:T(8,128)(2,1)S(1)}, bf16[1024,1536]{1,0:T(8,128)(2,1)}) %tuple.268), branch_computations={%region_47.48_spmd, %region_48.49_spmd} | conditional | flops 1208353792 | bytes 11011906 | solution.py:39
  223.9 4.7 %broadcast.380 = f32[1536,1536]{1,0:T(8,128)} broadcast(f32[]{:T(128)} %constant.76.clone), dimensions={} | broadcast | bytes 9437188 | tf_op jit(solution)/shard_map/broadcast.53
  228.7 3.4 conditional.47
  232.1 0.0 slice-start
  232.1 0.0 slice-start.1
  232.1 8.0 %fusion.192 = f32[1536,1536]{0,1:T(8,128)} fusion(bf16[1536,256]{1,0:T(8,128)(2,1)} %get-tuple-element.441, bf16[1536,1536]{1,0:T(8,128)(2,1)} %param.56, f32[1536,1536]{1,0:T(8,128)} %get-tuple-element.462, f32[]{:T(128)S(6)} %convert_element_type.142), kind=kOutput, calls=%fused_computation.235 | convolution fusion | flops 1217396736 | bytes 16515076 | tf_op jit(solution)/shard_map/dot_general | solution.py:86
  240.1 0.0 copy-done.2
  240.1 7.9 %fusion.195 = f32[1536,1536]{0,1:T(8,128)} fusion(f32[1536,1536]{0,1:T(8,128)} %fusion.192, bf16[1536,256]{1,0:T(8,128)(2,1)S(1)} %copy-done.2, bf16[1536,1536]{1,0:T(8,128)(2,1)} %param.56, f32[1536,1536]{1,0:T(8,128)} %get-tuple-element.466, f32[]{:T(128)S(6)} %convert_element_type.149), kind=kOutput, calls=%fused_computation.236 | convolution fusion | flops 1217396736 | bytes 16515076 | tf_op jit(solution)/shard_map/dot_general | solution.py:86
  248.0 0.0 slice-start.5
  248.0 0.0 slice-start.6
  248.0 0.0 slice-start.7
  248.1 5.4 %fusion.198 = f32[1536,1536]{0,1:T(8,128)} fusion(f32[1536,1536]{0,1:T(8,128)} %fusion.195, bf16[1536,256]{1,0:T(8,128)(2,1)S(1)} %copy-done.2, bf16[1536,1536]{1,0:T(8,128)(2,1)} %param.56, f32[1536,1536]{1,0:T(8,128)S(1)} %bitcast.26, f32[]{:T(128)S(6)} %convert_element_type.155), kind=kOutput, calls=%fused_computation.237 | convolution fusion | flops 1217396736 | bytes 16515076 | tf_op jit(solution)/shard_map/dot_general | solution.py:86
  253.4 0.0 slice-done.3
  253.4 0.0 slice-start.8
  253.4 0.0 slice-start.9
  253.4 0.0 slice-start.10
  253.5 5.6 %fusion.201 = f32[1536,1536]{0,1:T(8,128)} fusion(f32[1536,1536]{0,1:T(8,128)} %fusion.198, bf16[1536,256]{1,0:T(8,128)(2,1)} %get-tuple-element.441, bf16[1536,1536]{1,0:T(8,128)(2,1)} %param.56, f32[1536,1536]{1,0:T(8,128)S(1)} %bitcast.28, f32[]{:T(128)S(6)} %convert_element_type.161), kind=kOutput, calls=%fused_computation.238 | convolution fusion | flops 1217396736 | bytes 16515076 | tf_op jit(solution)/shard_map/dot_general | solution.py:86
  259.0 0.0 slice-done.6
  259.0 0.0 slice-done.8
  259.0 0.0 slice-start.11
  259.1 0.0 copy-start.3
  259.1 5.6 %fusion.204 = f32[1536,1536]{0,1:T(8,128)} fusion(f32[1536,1536]{0,1:T(8,128)} %fusion.201, bf16[1536,256]{1,0:T(8,128)(2,1)} %get-tuple-element.441, bf16[1536,1536]{1,0:T(8,128)(2,1)} %param.56, f32[1536,1536]{1,0:T(8,128)S(1)} %bitcast.30, f32[]{:T(128)S(6)} %convert_element_type.167), kind=kOutput, calls=%fused_computation.239 | convolution fusion | flops 1217396736 | bytes 16515076 | tf_op jit(solution)/shard_map/dot_general | solution.py:86
  264.7 0.0 slice-done.9
  264.7 5.2 %fusion.207 = f32[1536,1536]{0,1:T(8,128)} fusion(f32[1536,1536]{0,1:T(8,128)} %fusion.204, bf16[1536,256]{1,0:T(8,128)(2,1)S(1)} %copy-done.3, bf16[1536,1536]{1,0:T(8,128)(2,1)} %param.56, f32[1536,1536]{1,0:T(8,128)S(1)} %bitcast.32, f32[]{:T(128)S(6)} %convert_element_type.173), kind=kOutput, calls=%fused_computation.240 | convolution fusion | flops 1217396736 | bytes 16515076 | tf_op jit(solution)/shard_map/dot_general | solution.py:86
  269.9 0.0 reduce-scatter.3.cloned.1.call-update
  269.9 0.0 reduce-scatter.5.cloned.1.call-start
  270.0 160.6 %reduce-scatter.3.cloned.1.call-done = f32[384,1536]{0,1:T(8,128)} async-done(((f32[1536,1536]{0,1:T(8,128)}), f32[384,1536]{0,1:T(8,128)}) %reduce-scatter.3.cloned.1.call-update) | async-done | bytes 2359312 | tf_op jit(solution)/shard_map/reduce_scatter | solution.py:83
  430.6 1.8 convert_element_type.175
  432.4 1.5 copy.6
  433.9 0.0 reduce-scatter.5.cloned.1.call-update
  433.9 22.7 %reduce-scatter.5.cloned.1.call-done = bf16[384,6,1,128]{3,0,1,2:T(8,128)(2,1)} async-done(((bf16[384,6,2,128]{3,0,1,2:T(8,128)(2,1)}), bf16[384,6,1,128]{3,0,1,2:T(8,128)(2,1)}) %reduce-scatter.5.cloned.1.call-update) | async-done | bytes 589840 | tf_op jit(solution)/shard_map/reduce_scatter | solution.py:96
  (41 shorter events, 0.1 us)
Async XLA Ops:
  6.5 81.8 %copy-start.1 = (s32[6]{0:T(128)S(1)}, s32[6]{0:T(128)}, u32[]{:S(2)}) copy-start(s32[6]{0:T(128)} %param.57) | copy-start | bytes 76
  6.5 77.8 %all-gather.2.cloned.1.call-start = ((), (), s32[]{:S(2)}) async-start(), calls=%async_computation.2 | async-start | bytes 3932160 | tf_op jit(solution)/shard_map/all_gather | solution.py:67
  20.3 148.1 %all-reduce.4.cloned.1.call-start = ((), (), s32[]{:S(2)}) async-start(), calls=%async_computation.5 | async-start | bytes 7864320 | tf_op jit(solution)/shard_map/psum | solution.py:12
  84.3 84.2 %copy-start = (bf16[1024,1536]{1,0:T(8,128)(2,1)S(1)}, bf16[1024,1536]{1,0:T(8,128)(2,1)}, u32[]{:S(2)}) copy-start(bf16[1024,1536]{1,0:T(8,128)(2,1)} %all-gather.2.cloned.1.call-done) | copy-start | bytes 9437188
  88.3 342.3 %reduce-scatter.3.cloned.1.call-start = ((), (), s32[]{:S(2)}) async-start(), calls=%async_computation.3 | async-start | bytes 11796480 | tf_op jit(solution)/shard_map/reduce_scatter | solution.py:83
  232.1 8.0 %copy-start.2 = (bf16[1536,256]{1,0:T(8,128)(2,1)S(1)}, bf16[1536,256]{1,0:T(8,128)(2,1)}, u32[]{:S(2)}) copy-start(bf16[1536,256]{1,0:T(8,128)(2,1)} %get-tuple-element.441) | copy-start | bytes 2359300
  232.1 15.9 %slice-start = ((s8[9437184]{0:T(1024)(128)(4,1)}), s8[4194304]{0:T(1024)(128)(4,1)S(1)}, s32[]{:S(2)}) async-start(s8[9437184]{0:T(1024)(128)(4,1)} %bitcast.25), calls=%async_computation.6 | async-start | bytes 8388608
  232.1 15.9 %slice-start.1 = ((s8[9437184]{0:T(1024)(128)(4,1)}), s8[4194304]{0:T(1024)(128)(4,1)S(1)}, s32[]{:S(2)}) async-start(s8[9437184]{0:T(1024)(128)(4,1)} %bitcast.25), calls=%async_computation.7 | async-start | bytes 8388608
  240.1 7.9 %slice-start.2 = ((s8[9437184]{0:T(1024)(128)(4,1)}), s8[1048576]{0:T(1024)(128)(4,1)S(1)}, s32[]{:S(2)}) async-start(s8[9437184]{0:T(1024)(128)(4,1)} %bitcast.25), calls=%async_computation.8 | async-start | bytes 2097152
  240.1 13.3 %slice-start.3 = ((s8[9437184]{0:T(1024)(128)(4,1)}), s8[4194304]{0:T(1024)(128)(4,1)S(1)}, s32[]{:S(2)}) async-start(s8[9437184]{0:T(1024)(128)(4,1)} %bitcast.27), calls=%async_computation.9 | async-start | bytes 8388608
  240.1 13.3 %slice-start.4 = ((s8[9437184]{0:T(1024)(128)(4,1)}), s8[4194304]{0:T(1024)(128)(4,1)S(1)}, s32[]{:S(2)}) async-start(s8[9437184]{0:T(1024)(128)(4,1)} %bitcast.27), calls=%async_computation.10 | async-start | bytes 8388608
  248.0 5.4 %slice-start.5 = ((s8[9437184]{0:T(1024)(128)(4,1)}), s8[1048576]{0:T(1024)(128)(4,1)S(1)}, s32[]{:S(2)}) async-start(s8[9437184]{0:T(1024)(128)(4,1)} %bitcast.27), calls=%async_computation.11 | async-start | bytes 2097152
  248.0 11.0 %slice-start.6 = ((s8[9437184]{0:T(1024)(128)(4,1)}), s8[4194304]{0:T(1024)(128)(4,1)S(1)}, s32[]{:S(2)}) async-start(s8[9437184]{0:T(1024)(128)(4,1)} %bitcast.29), calls=%async_computation.12 | async-start | bytes 8388608
  248.0 11.0 %slice-start.7 = ((s8[9437184]{0:T(1024)(128)(4,1)}), s8[4194304]{0:T(1024)(128)(4,1)S(1)}, s32[]{:S(2)}) async-start(s8[9437184]{0:T(1024)(128)(4,1)} %bitcast.29), calls=%async_computation.13 | async-start | bytes 8388608
  253.4 5.6 %slice-start.8 = ((s8[9437184]{0:T(1024)(128)(4,1)}), s8[1048576]{0:T(1024)(128)(4,1)S(1)}, s32[]{:S(2)}) async-start(s8[9437184]{0:T(1024)(128)(4,1)} %bitcast.29), calls=%async_computation.14 | async-start | bytes 2097152
  253.4 11.3 %slice-start.9 = ((s8[9437184]{0:T(1024)(128)(4,1)}), s8[4194304]{0:T(1024)(128)(4,1)S(1)}, s32[]{:S(2)}) async-start(s8[9437184]{0:T(1024)(128)(4,1)} %bitcast.31), calls=%async_computation.15 | async-start | bytes 8388608
  253.4 11.3 %slice-start.10 = ((s8[9437184]{0:T(1024)(128)(4,1)}), s8[4194304]{0:T(1024)(128)(4,1)S(1)}, s32[]{:S(2)}) async-start(s8[9437184]{0:T(1024)(128)(4,1)} %bitcast.31), calls=%async_computation.16 | async-start | bytes 8388608
  259.0 5.7 %slice-start.11 = ((s8[9437184]{0:T(1024)(128)(4,1)}), s8[1048576]{0:T(1024)(128)(4,1)S(1)}, s32[]{:S(2)}) async-start(s8[9437184]{0:T(1024)(128)(4,1)} %bitcast.31), calls=%async_computation.17 | async-start | bytes 2097152
  259.1 5.7 %copy-start.3 = (bf16[1536,256]{1,0:T(8,128)(2,1)S(1)}, bf16[1536,256]{1,0:T(8,128)(2,1)}, u32[]{:S(2)}) copy-start(bf16[1536,256]{1,0:T(8,128)(2,1)} %get-tuple-element.441) | copy-start | bytes 2359300
  269.9 186.7 %reduce-scatter.5.cloned.1.call-start = ((), (), s32[]{:S(2)}) async-start(), calls=%async_computation.4 | async-start | bytes 1769472 | tf_op jit(solution)/shard_map/reduce_scatter | solution.py:96
Sparse Core Ops, SparseCore 0:
  20.5 63.7 all-gather.1
  88.4 80.0 all-reduce.3
  270.0 160.5 reduce-scatter.2
  434.0 22.5 reduce-scatter.4
where the time goes:
time: 471 us; the launch traced here: 464 us
  waiting for transfers between devices  309 us (66%)
  matrix products  77.6 us (16%)
  between operations  29.1 us (6%)
  local copies, waits for them, and re-layouts  22.1 us (5%)
  other arithmetic  13.5 us (3%)
  blocking collectives  8.37 us (2%)
    reduce_scatter x1, waiting for transfers between devices, shards(): lax.psum_scatter(jnp.concatenate([jnp.dot(hadamard, col_res, preferred_el...  161 us
    psum x1, waiting for transfers between devices, broadcast(): return lax.psum(jnp.where(mine, shard, jnp.zeros_like(shard)), axis)  63.3 us
    all_gather x1, waiting for transfers between devices, shards(): row_geno = lax.all_gather(standard, 'col', axis=0, tiled=True)  61.8 us
    dot_general x5, matrix products, gram_update(): lax.dot_general(left_block, right_block, (((0,), (0,)), ((), ())), prefer...  40 us
    dot_general x6, matrix products, shards(): jnp.dot(hadamard, col_res, preferred_element_type=jnp.float32)  37.6 us
    reduce_scatter x1, waiting for transfers between devices, shards(): lax.psum_scatter(shaped.astype(jnp.bfloat16), 'segment', scatter_dimensio...  22.7 us
    another operation x4, local copies, waits for them, and re-layouts  19.2 us
  transfers between devices with their start and end apart: 4, of which 4 were waited for; matrix products, arithmetic and copies ran while one was open for 1% of the time, Pallas kernels for 0%

commit v1 on v0

v1 whole, which is shorter than its diff:
```python
import functools

import jax
import jax.numpy as jnp
from jax import lax
from jax.experimental import pallas as pl
from jax.experimental.pallas import tpu as pltpu
from jax.sharding import PartitionSpec as P

BLOCK = 256
COL_TILE = 512


def spread(piece, row, col, n_row, n_col):
    have = piece
    bit = n_row // 2
    while bit:
        pairs = [
            (r * n_col + c, (r ^ bit) * n_col + c)
            for c in range(n_col)
            for r in range(n_row)
            if (r ^ c) & (2 * bit - 1) == 0
        ]
        got = lax.ppermute(have, ("row", "col"), pairs)
        have = jnp.where(((row ^ col) & (2 * bit - 1)) == bit, got, have)
        bit //= 2
    return have


def slot_kernel(shift, n, segments, info, inverse, *refs):
    rows, cols = refs[:n], refs[n : 2 * n]
    grm, res, own_out, send_out = refs[2 * n : 2 * n + 4]
    row_buf, col_buf, left_buf, grm_buf, res_buf, total, sems = refs[2 * n + 4 :]
    chunk, variants = row_buf.shape
    tile = col_buf.shape[0]
    share = variants // n
    col_tile = min(COL_TILE, tile)
    half = own_out.shape[2]
    col = info[2 * segments]
    first = pl.multiple_of(lax.rem(col + n - shift, n) * chunk, chunk)
    copies = []
    for s in range(n):
        at = pl.multiple_of(lax.rem(col + n - s, n) * share, share)
        copies.append(
            pltpu.make_async_copy(
                rows[s].at[pl.ds(first, chunk), :], row_buf.at[:, pl.ds(at, share)], sems.at[2 * s]
            )
        )
        copies.append(
            pltpu.make_async_copy(cols[s], col_buf.at[:, pl.ds(at, share)], sems.at[2 * s + 1])
        )
    copies.append(pltpu.make_async_copy(grm.at[pl.ds(first, chunk), :], grm_buf, sems.at[2 * n]))
    copies.append(pltpu.make_async_copy(res, res_buf, sems.at[2 * n + 1]))
    for copy in copies:
        copy.start()
    for copy in copies:
        copy.wait()

    def segment(s, carry):
        lower, upper = info[s], info[segments + s]
        first_block = lower // BLOCK
        blocks = (upper + BLOCK - 1) // BLOCK - first_block
        start = pl.multiple_of(first_block * BLOCK, BLOCK)

        @pl.when(upper <= lower)
        def _():
            own_out[s] = jnp.zeros(own_out.shape[1:], own_out.dtype)
            send_out[s] = jnp.zeros(send_out.shape[1:], send_out.dtype)

        for m in range(1, variants // BLOCK + 1):

            @pl.when((upper > lower) & (blocks == m))
            def _(m=m):
                depth = m * BLOCK
                index = start + lax.broadcasted_iota(jnp.int32, (chunk, depth), 1)
                left = row_buf[:, pl.ds(start, depth)]
                left_buf[:, :depth] = jnp.where(
                    (index >= lower) & (index < upper), left, jnp.zeros_like(left)
                )
                for j in range(tile // col_tile):
                    span = slice(j * col_tile, (j + 1) * col_tile)
                    gram = lax.dot_general(
                        left_buf[:, :depth],
                        col_buf[span, pl.ds(start, depth)],
                        (((1,), (1,)), ((), ())),
                        preferred_element_type=jnp.float32,
                    )
                    hadamard = (gram * grm_buf[:, span].astype(jnp.float32)).astype(jnp.bfloat16)
                    part = jnp.dot(hadamard, res_buf[span, :], preferred_element_type=jnp.float32)
                    if j == 0:
                        total[...] = part
                    else:
                        total[...] += part
                scores = total[...] * inverse[s]
                own_out[s] = scores[:, :half]
                send_out[s] = scores[:, half:].astype(send_out.dtype)

        return carry

    lax.fori_loop(0, segments, segment, 0)


def slot(shift, info, inverse, rows, cols, grm, res, segments, half):
    n = len(rows)
    tile, share = rows[0].shape
    chunk, variants = tile // n, share * n
    width = res.shape[1]
    any_spec = pl.BlockSpec(memory_space=pl.ANY)
    smem = pl.BlockSpec(memory_space=pltpu.SMEM)
    vmem = pl.BlockSpec(memory_space=pltpu.VMEM)
    return pl.pallas_call(
        functools.partial(slot_kernel, shift, n, segments),
        out_shape=(
            jax.ShapeDtypeStruct((segments, chunk, half), jnp.float32),
            jax.ShapeDtypeStruct((segments, chunk, width - half), jnp.bfloat16),
        ),
        in_specs=[smem, smem] + [any_spec] * (2 * n + 2),
        out_specs=(vmem, vmem),
        scratch_shapes=[
            pltpu.VMEM((chunk, variants), jnp.bfloat16),
            pltpu.VMEM((tile, variants), jnp.bfloat16),
            pltpu.VMEM((chunk, variants), jnp.bfloat16),
            pltpu.VMEM((chunk, tile), jnp.bfloat16),
            pltpu.VMEM((tile, width), jnp.bfloat16),
            pltpu.VMEM((chunk, width), jnp.float32),
            pltpu.SemaphoreType.DMA((2 * n + 2,)),
        ],
        compiler_params=pltpu.CompilerParams(vmem_limit_bytes=40 << 20),
        cost_estimate=pl.CostEstimate(
            flops=2 * chunk * tile * (variants + 4 * width),
            bytes_accessed=tile * variants * 2 + chunk * tile * 2 + tile * width * 2,
            transcendentals=0,
        ),
    )(info, inverse, *rows, *cols, grm, res)


def shards(dosage, missing, residuals, global_grm, seg_counts):
    n_seg, n_row, n_col = (lax.axis_size(a) for a in ("segment", "row", "col"))
    group, row, col = (lax.axis_index(a) for a in ("segment", "row", "col"))
    segments = seg_counts.shape[0]
    share, tile = dosage.shape
    width = residuals.shape[1]
    half = width // n_seg
    half_vars = share * n_col

    observed = (1 - missing).astype(jnp.float32)
    alt_local = jnp.sum(dosage * observed, axis=1)
    obs_local = jnp.sum(observed, axis=1)
    alt_total, obs_total = lax.psum((alt_local, obs_local), "row")
    allele_freq = (alt_total + 1.0) / (2.0 * obs_total + 2.0)
    allele_spread = jnp.sqrt(2.0 * allele_freq * (1.0 - allele_freq))
    standard = (observed * (dosage - 2.0 * allele_freq[:, None]) / allele_spread[:, None]).astype(
        jnp.bfloat16
    )

    seg_starts = jnp.cumsum(seg_counts) - seg_counts
    lower = jnp.clip(seg_starts - group * half_vars, 0, half_vars)
    upper = jnp.clip(seg_starts + seg_counts - group * half_vars, 0, half_vars)
    info = jnp.concatenate([lower, upper, col[None]]).astype(jnp.int32)
    inverse = 1.0 / seg_counts.astype(jnp.float32)

    parts = residuals.reshape(tile, n_seg, half)
    res = spread(jnp.roll(parts, -group, axis=1).reshape(tile, width), row, col, n_row, n_col)

    ring = [(i, (i + 1) % n_col) for i in range(n_col)]
    rows = [standard.T]
    for _ in range(n_col - 1):
        rows.append(lax.ppermute(rows[-1], "col", ring))
    cols = [spread(piece, row, col, n_row, n_col) for piece in rows]

    carried = None
    for k in range(1, n_col + 1):
        own, send = slot(k, info, inverse, rows, cols, global_grm, res, segments, half)
        got = own
        for j in range(1, n_seg):
            mine = send[:, :, (j - 1) * half : j * half]
            got = got + lax.ppermute(
                mine, "segment", [(i, (i + j) % n_seg) for i in range(n_seg)]
            ).astype(jnp.float32)
        if carried is not None:
            got = got + carried.astype(jnp.float32)
        got = got.astype(jnp.bfloat16)
        carried = lax.ppermute(got, "col", ring) if k < n_col else got
    return carried


def solution(mesh):
    placed = (
        P(("segment", "col"), "row"),
        P(("segment", "col"), "row"),
        P("row", None),
        P("row", "col"),
        P(),
    )
    return jax.shard_map(
        shards,
        mesh=mesh,
        in_specs=placed,
        out_specs=P(None, ("row", "col"), "segment"),
        check_vma=False,
    )
```

time: 471 us -> 162 us (0.34); the launches traced: 464 us -> 162 us
  waiting for transfers between devices: 309 us -> 80.1 us
  matrix products: 77.6 us -> 0 us
  Pallas kernels: 0 us -> 29.5 us
  between operations: 29.1 us -> 0.41 us
  starting transfers between devices: 0.13 us -> 28.2 us
  local copies, waits for them, and re-layouts: 22.1 us -> 7.62 us
  other arithmetic: 13.5 us -> 7.64 us
    reduce_scatter x2 -> x0, waiting for transfers between devices: 183 us -> none  [the longest x1 161 us: shards(): lax.psum_scatter(jnp.concatenate([jnp.dot(hadamard, col_res, preferred_el...]
    ppermute x0 -> x20, waiting for transfers between devices: none -> 80.1 us  [the longest x3 31.8 us: shards(): rows.append(lax.ppermute(rows[-1], 'col', ring))]
    dot_general x11 -> x0, matrix products: 77.6 us -> none  [the longest x5 40 us: gram_update(): lax.dot_general(left_block, right_block, (((0,), (0,)), ((), ())), prefer...]
    psum x1 -> x0, waiting for transfers between devices: 63.3 us -> none  [broadcast(): return lax.psum(jnp.where(mine, shard, jnp.zeros_like(shard)), axis)]
    all_gather x1 -> x0, waiting for transfers between devices: 61.8 us -> none  [shards(): row_geno = lax.all_gather(standard, 'col', axis=0, tiled=True)]
    pallas_call x0 -> x4, Pallas kernels: none -> 29.5 us  [slot(): pl.pallas_call(functools.partial(slot_kernel, shift, n, segments), out_sh...]
    ppermute x0 -> x20, starting transfers between devices: none -> 28.2 us  [the longest x10 25.8 us: spread(): got = lax.ppermute(have, ('row', 'col'), pairs)]
    another operation x4 -> x0, local copies, waits for them, and re-layouts: 19.2 us -> none
  transfers between devices with their start and end apart: 4 -> 20, of which waited for: 4 -> 12; matrix products, arithmetic and copies ran while one was open for 1% -> 5% of each run, Pallas kernels for 0% -> 14%
where the time goes in v1:
time: 162 us
  waiting for transfers between devices  80.1 us (49%)
  Pallas kernels  29.5 us (18%)
  starting transfers between devices  28.2 us (17%)
  blocking collectives  8.34 us (5%)
  other arithmetic  7.64 us (5%)
  local copies, waits for them, and re-layouts  7.62 us (5%)
    ppermute x3, waiting for transfers between devices, shards(): rows.append(lax.ppermute(rows[-1], 'col', ring))  31.8 us
    pallas_call x4, Pallas kernels, slot(): pl.pallas_call(functools.partial(slot_kernel, shift, n, segments), out_sh...  29.5 us
    ppermute x10, starting transfers between devices, spread(): got = lax.ppermute(have, ('row', 'col'), pairs)  25.8 us
    ppermute x3, waiting for transfers between devices, shards(): carried = lax.ppermute(got, 'col', ring) if k < n_col else got  19.6 us
    ppermute x4, waiting for transfers between devices, shards(): lax.ppermute(mine, 'segment', [(i, (i + j) % n_seg) for i in range(n_seg)])  19.4 us
    ppermute x10, waiting for transfers between devices, spread(): got = lax.ppermute(have, ('row', 'col'), pairs)  9.22 us
    psum x1, blocking collectives, shards(): alt_total, obs_total = lax.psum((alt_local, obs_local), 'row')  8.34 us
    unnamed x11, local copies, waits for them, and re-layouts  5.6 us
  transfers between devices with their start and end apart: 20, of which 12 were waited for; matrix products, arithmetic and copies ran while one was open for 5% of the time, Pallas kernels for 14%

profile of v1, /device:TPU:0, one launch (start us, length us, event | category | flops | bytes accessed | tf_op | source)
XLA Modules:
  0.0 161.7 jit_solution(9585257729543780801)
XLA Ops:
  0.0 1.9 %copy.8 = f32[256,1536]{0,1:T(8,128)S(1)} copy(f32[256,1536]{1,0:T(8,128)} %param.5) | data formatting | bytes 3145728 | tf_op args[0]
  1.9 1.9 %copy.6 = s32[256,1536]{0,1:T(8,128)S(1)} copy(s32[256,1536]{1,0:T(8,128)} %param.6) | data formatting | bytes 3145728 | tf_op args[1]
  3.8 0.3 multiply_reduce_fusion
  4.1 0.8 copy-done
  4.9 8.3 %all-reduce = (f32[256]{0:T(256)S(1)}, f32[256]{0:T(256)S(1)}) all-reduce(f32[256]{0:T(256)S(1)} %get-tuple-element.22, f32[256]{0:T(256)S(1)} %get-tuple-element.21), channel_id=1, replica_groups=mesh['segment'=2,'row'=4,'col'=4] {'row'}, use_global_device_ids=true, to_apply=%region_4.0 | all-reduce | flops 512 | bytes 4096 | tf_op jit(solution)/shard_map/psum | solution.py:149
  13.3 1.7 %fusion.1.refs_0_ = bf16[1536,256]{1,0:T(8,128)(2,1)S(1)} fusion(f32[256]{0:T(256)S(1)} %multiply_sqrt_fusion, f32[256,1536]{0,1:T(8,128)S(1)} %copy.8, f32[256]{0:T(256)S(1)} %get-tuple-element.25, s32[256,1536]{0,1:T(8,128)} %copy-done), kind=kLoop, calls=%fused_computation.11 | loop fusion | flops 2359296 | bytes 3934208 | tf_op jit(solution)/shard_map/transpose | solution.py:166
  15.0 1.6 %collective-permute-start = (bf16[1536,256]{1,0:T(8,128)(2,1)S(1)}, bf16[1536,256]{1,0:T(8,128)(2,1)S(1)}, u32[]{:S(2)}, u32[]{:S(2)}) collective-permute-start(bf16[1536,256]{1,0:T(8,128)(2,1)S(1)} %fusion.1.refs_0_), channel_id=1, source_target_pairs={{0,1},{1,2},{2,3},{3,0},{4,5},{5,6},{6,7},{7,4},{8,9},{9,10},{10,1... | collective-permute-start | bytes 2359304 | tf_op jit(solution)/shard_map/ppermute | solution.py:168
  16.6 3.3 %collective-permute-start.3 = (bf16[1536,256]{1,0:T(8,128)(2,1)S(1)}, bf16[1536,256]{1,0:T(8,128)(2,1)}, u32[]{:S(2)}, u32[]{:S(2)}) collective-permute-start(bf16[1536,256]{1,0:T(8,128)(2,1)S(1)} %fusion.1.refs_0_), channel_id=1, source_target_pairs={{0,8},{5,13},{10,2},{15,7},{16,24},{21,29},{26,18},{31,23}} | collective-permute-start | bytes 2359304 | tf_op jit(solution)/shard_map/ppermute | solution.py:24
  19.9 2.0 %reshape.37 = bf16[1536,2,128]{2,1,0:T(2,128)(2,1)S(1)} reshape(bf16[1536,256]{1,0:T(8,128)(2,1)} %param.7) | data formatting | bytes 1572864 | tf_op jit(solution)/shard_map/reshape | solution.py:162
  21.9 0.0 copy-start.1
  21.9 2.9 %fusion = bf16[1536,2,128]{2,1,0:T(2,128)(2,1)S(1)} fusion(s32[]{:T(128)S(6)} %select_n.70, bf16[1536,2,128]{2,1,0:T(2,128)(2,1)S(1)} %reshape.37), kind=kLoop, calls=%fused_computation.9 | loop fusion | flops 1572864 | bytes 1572868 | tf_op jit(solution)/shard_map/jit(_roll_dynamic)/concatenate | solution.py:163
  24.8 1.0 copy.13
  25.8 1.3 collective-permute-start.11
  27.2 0.2 reduce-window.9
  27.4 0.1 pad_add_fusion.info
  27.5 7.5 %collective-permute-done.refs_1_ = bf16[1536,256]{1,0:T(8,128)(2,1)S(1)} collective-permute-done((bf16[1536,256]{1,0:T(8,128)(2,1)S(1)}, bf16[1536,256]{1,0:T(8,128)(2,1)S(1)}, u32[]{:S(2)}, u32[]{:S(2)}) %collective-permute-start) | collective-permute-done | bytes 786464 | tf_op jit(solution)/shard_map/ppermute | solution.py:168
  35.0 3.5 %collective-permute-start.5 = (bf16[1536,256]{1,0:T(8,128)(2,1)S(1)}, bf16[1536,256]{1,0:T(8,128)(2,1)S(1)}, u32[]{:S(2)}, u32[]{:S(2)}) collective-permute-start(bf16[1536,256]{1,0:T(8,128)(2,1)S(1)} %collective-permute-done.refs_1_), channel_id=1, source_target_pairs={{0,8},{5,13},{10,2},{15,7},{16,24},{21,29},{26,18},{31,23}} | collective-permute-start | bytes 2359304 | tf_op jit(solution)/shard_map/ppermute | solution.py:24
  38.5 0.1 broadcast_select_fusion.4
  38.6 1.3 collective-permute-start.4
  39.9 0.1 broadcast_select_fusion
  40.0 1.3 collective-permute-start.12
  41.4 12.5 %collective-permute-done.1.refs_2_ = bf16[1536,256]{1,0:T(8,128)(2,1)S(1)} collective-permute-done((bf16[1536,256]{1,0:T(8,128)(2,1)S(1)}, bf16[1536,256]{1,0:T(8,128)(2,1)S(1)}, u32[]{:S(2)}, u32[]{:S(2)}) %collective-permute-start.1) | collective-permute-done | bytes 786464 | tf_op jit(solution)/shard_map/ppermute | solution.py:168
  54.0 0.1 broadcast_select_fusion.3
  54.0 1.3 collective-permute-start.6
  55.4 4.8 %collective-permute-start.7 = (bf16[1536,256]{1,0:T(8,128)(2,1)S(1)}, bf16[1536,256]{1,0:T(8,128)(2,1)S(1)}, u32[]{:S(2)}, u32[]{:S(2)}) collective-permute-start(bf16[1536,256]{1,0:T(8,128)(2,1)S(1)} %collective-permute-done.1.refs_2_), channel_id=1, source_target_pairs={{0,8},{5,13},{10,2},{15,7},{16,24},{21,29},{26,18},{31,23}} | collective-permute-start | bytes 2359304 | tf_op jit(solution)/shard_map/ppermute | solution.py:24
  60.2 0.0 slice-start
  60.2 0.1 broadcast_select_fusion.9.refs_4_
  60.3 11.7 %collective-permute-done.2.refs_3_ = bf16[1536,256]{1,0:T(8,128)(2,1)S(1)} collective-permute-done((bf16[1536,256]{1,0:T(8,128)(2,1)S(1)}, bf16[1536,256]{1,0:T(8,128)(2,1)S(1)}, u32[]{:S(2)}, u32[]{:S(2)}) %collective-permute-start.2) | collective-permute-done | bytes 786464 | tf_op jit(solution)/shard_map/ppermute | solution.py:168
  72.0 6.0 %collective-permute-start.9 = (bf16[1536,256]{1,0:T(8,128)(2,1)S(1)}, bf16[1536,256]{1,0:T(8,128)(2,1)S(1)}, u32[]{:S(2)}, u32[]{:S(2)}) collective-permute-start(bf16[1536,256]{1,0:T(8,128)(2,1)S(1)} %collective-permute-done.2.refs_3_), channel_id=1, source_target_pairs={{0,8},{5,13},{10,2},{15,7},{16,24},{21,29},{26,18},{31,23}} | collective-permute-start | bytes 2359304 | tf_op jit(solution)/shard_map/ppermute | solution.py:24
  78.0 0.0 collective-permute-done.12
  78.0 0.1 broadcast_select_fusion.5.refs_9_
  78.1 0.1 broadcast_select_fusion.2
  78.2 0.0 slice-start.1
  78.2 1.5 collective-permute-start.8
  79.7 7.7 %collective-permute-done.9 = bf16[1536,256]{1,0:T(8,128)(2,1)S(1)} collective-permute-done((bf16[1536,256]{1,0:T(8,128)(2,1)S(1)}, bf16[1536,256]{1,0:T(8,128)(2,1)S(1)}, u32[]{:S(2)}, u32[]{:S(2)}) %collective-permute-start.9) | collective-permute-done | bytes 786464 | tf_op jit(solution)/shard_map/ppermute | solution.py:24
  87.5 0.1 broadcast_select_fusion.1
  87.5 1.5 collective-permute-start.10
  89.1 0.0 collective-permute-done.6
  89.1 0.1 broadcast_select_fusion.8.refs_5_
  89.2 0.1 broadcast_select_fusion.7.refs_6_
  89.3 1.5 collective-permute-done.10
  90.7 0.1 broadcast_select_fusion.6.refs_7_
  90.8 7.4 %shard_map.58 = (f32[6,384,128]{2,1,0:T(8,128)S(1)}, bf16[6,384,128]{2,1,0:T(8,128)(2,1)S(1)}) custom-call(s32[13]{0:T(128)S(1)} %pad_add_fusion.info, f32[6]{0:T(128)S(1)} %convert_divide_fusion.inverse, bf16[1536,256]{1,0:T(8,128)(2,1)S(1)} %fusion.1.refs_0_, bf16[1536,256]{1,0:T(8,128)(2,1)S(1)} %collective-permute-done.refs_1_, ...), custom_call_target="tpu_custom_call" | custom-call | flops 2415919104 | bytes 5111808 | tf_op jit(solution)/shard_map/pallas_call | solution.py:111
  98.2 0.1 collective-permute-start.16
  98.3 7.4 %shard_map.57 = (f32[6,384,128]{2,1,0:T(8,128)S(1)}, bf16[6,384,128]{2,1,0:T(8,128)(2,1)S(1)}) custom-call(s32[13]{0:T(128)S(1)} %pad_add_fusion.info, f32[6]{0:T(128)S(1)} %convert_divide_fusion.inverse, bf16[1536,256]{1,0:T(8,128)(2,1)S(1)} %fusion.1.refs_0_, bf16[1536,256]{1,0:T(8,128)(2,1)S(1)} %collective-permute-done.refs_1_, ...), custom_call_target="tpu_custom_call" | custom-call | flops 2415919104 | bytes 5111808 | tf_op jit(solution)/shard_map/pallas_call | solution.py:111
  105.7 0.1 collective-permute-start.15
  105.8 8.7 %collective-permute-done.16 = bf16[6,384,128]{2,1,0:T(8,128)(2,1)S(1)} collective-permute-done((bf16[6,384,128]{2,1,0:T(8,128)(2,1)S(1)}, bf16[6,384,128]{2,1,0:T(8,128)(2,1)S(1)}, u32[]{:S(2)}, u32[]{:S(2)}) %collective-permute-start.16) | collective-permute-done | bytes 589856 | tf_op jit(solution)/shard_map/ppermute | solution.py:177
  114.5 0.1 add_convert_fusion.3
  114.6 0.3 collective-permute-start.17
  114.9 7.4 %shard_map.56 = (f32[6,384,128]{2,1,0:T(8,128)S(1)}, bf16[6,384,128]{2,1,0:T(8,128)(2,1)S(1)}) custom-call(s32[13]{0:T(128)S(1)} %pad_add_fusion.info, f32[6]{0:T(128)S(1)} %convert_divide_fusion.inverse, bf16[1536,256]{1,0:T(8,128)(2,1)S(1)} %fusion.1.refs_0_, bf16[1536,256]{1,0:T(8,128)(2,1)S(1)} %collective-permute-done.refs_1_, ...), custom_call_target="tpu_custom_call" | custom-call | flops 2415919104 | bytes 5111808 | tf_op jit(solution)/shard_map/pallas_call | solution.py:111
  122.2 0.1 collective-permute-start.14
  122.3 4.8 %collective-permute-done.15 = bf16[6,384,128]{2,1,0:T(8,128)(2,1)S(1)} collective-permute-done((bf16[6,384,128]{2,1,0:T(8,128)(2,1)S(1)}, bf16[6,384,128]{2,1,0:T(8,128)(2,1)S(1)}, u32[]{:S(2)}, u32[]{:S(2)}) %collective-permute-start.15) | collective-permute-done | bytes 589856 | tf_op jit(solution)/shard_map/ppermute | solution.py:177
  127.1 3.8 %collective-permute-done.17 = bf16[6,384,128]{2,1,0:T(8,128)(2,1)S(1)} collective-permute-done((bf16[6,384,128]{2,1,0:T(8,128)(2,1)S(1)}, bf16[6,384,128]{2,1,0:T(8,128)(2,1)S(1)}, u32[]{:S(2)}, u32[]{:S(2)}) %collective-permute-start.17) | collective-permute-done | bytes 589856 | tf_op jit(solution)/shard_map/ppermute | solution.py:183
  130.9 0.2 add_convert_fusion.2
  131.1 0.1 collective-permute-start.18
  131.1 7.4 %shard_map.55 = (f32[6,384,128]{2,1,0:T(8,128)S(1)}, bf16[6,384,128]{2,1,0:T(8,128)(2,1)S(1)}) custom-call(s32[13]{0:T(128)S(1)} %pad_add_fusion.info, f32[6]{0:T(128)S(1)} %convert_divide_fusion.inverse, bf16[1536,256]{1,0:T(8,128)(2,1)S(1)} %fusion.1.refs_0_, bf16[1536,256]{1,0:T(8,128)(2,1)S(1)} %collective-permute-done.refs_1_, ...), custom_call_target="tpu_custom_call" | custom-call | flops 2415919104 | bytes 5111808 | tf_op jit(solution)/shard_map/pallas_call | solution.py:111
  138.5 0.1 collective-permute-start.13
  138.6 0.6 collective-permute-done.14
  139.2 7.1 %collective-permute-done.18 = bf16[6,384,128]{2,1,0:T(8,128)(2,1)S(1)} collective-permute-done((bf16[6,384,128]{2,1,0:T(8,128)(2,1)S(1)}, bf16[6,384,128]{2,1,0:T(8,128)(2,1)S(1)}, u32[]{:S(2)}, u32[]{:S(2)}) %collective-permute-start.18) | collective-permute-done | bytes 589856 | tf_op jit(solution)/shard_map/ppermute | solution.py:183
  146.2 0.2 add_convert_fusion.1
  146.4 0.1 collective-permute-start.19
  146.5 5.4 %collective-permute-done.13 = bf16[6,384,128]{2,1,0:T(8,128)(2,1)S(1)} collective-permute-done((bf16[6,384,128]{2,1,0:T(8,128)(2,1)S(1)}, bf16[6,384,128]{2,1,0:T(8,128)(2,1)S(1)}, u32[]{:S(2)}, u32[]{:S(2)}) %collective-permute-start.13) | collective-permute-done | bytes 589856 | tf_op jit(solution)/shard_map/ppermute | solution.py:177
  151.9 8.8 %collective-permute-done.19 = bf16[6,384,128]{2,1,0:T(8,128)(2,1)S(1)} collective-permute-done((bf16[6,384,128]{2,1,0:T(8,128)(2,1)S(1)}, bf16[6,384,128]{2,1,0:T(8,128)(2,1)S(1)}, u32[]{:S(2)}, u32[]{:S(2)}) %collective-permute-start.19) | collective-permute-done | bytes 589856 | tf_op jit(solution)/shard_map/ppermute | solution.py:183
  160.7 1.0 add_convert_fusion
  (17 shorter events, 0.1 us)
Async XLA Ops:
  3.8 1.2 copy-start
  15.0 20.0 %collective-permute-start = (bf16[1536,256]{1,0:T(8,128)(2,1)S(1)}, bf16[1536,256]{1,0:T(8,128)(2,1)S(1)}, u32[]{:S(2)}, u32[]{:S(2)}) collective-permute-start(bf16[1536,256]{1,0:T(8,128)(2,1)S(1)} %fusion.1.refs_0_), channel_id=1, source_target_pairs={{0,1},{1,2},{2,3},{3,0},{4,5},{5,6},{6,7},{7,4},{8,9},{9,10},{10,1... | collective-permute-start | bytes 2359304 | tf_op jit(solution)/shard_map/ppermute | solution.py:168
  16.6 21.8 %collective-permute-start.3 = (bf16[1536,256]{1,0:T(8,128)(2,1)S(1)}, bf16[1536,256]{1,0:T(8,128)(2,1)}, u32[]{:S(2)}, u32[]{:S(2)}) collective-permute-start(bf16[1536,256]{1,0:T(8,128)(2,1)S(1)} %fusion.1.refs_0_), channel_id=1, source_target_pairs={{0,8},{5,13},{10,2},{15,7},{16,24},{21,29},{26,18},{31,23}} | collective-permute-start | bytes 2359304 | tf_op jit(solution)/shard_map/ppermute | solution.py:24
  21.9 5.3 %copy-start.1 = (s32[6]{0:T(128)S(1)}, s32[6]{0:T(128)}, u32[]{:S(2)}) copy-start(s32[6]{0:T(128)} %param.9) | copy-start | bytes 76
  25.8 14.1 %collective-permute-start.11 = (bf16[1536,256]{1,0:T(8,128)(2,1)}, bf16[1536,256]{1,0:T(8,128)(2,1)S(1)}, u32[]{:S(2)}, u32[]{:S(2)}) collective-permute-start(bf16[1536,256]{1,0:T(8,128)(2,1)} %bitcast.18), channel_id=1, source_target_pairs={{0,8},{5,13},{10,2},{15,7},{16,24},{21,29},{26,18},{31,23}} | collective-permute-start | bytes 2359304 | tf_op jit(solution)/shard_map/ppermute | solution.py:24
  35.0 19.0 %collective-permute-start.1 = (bf16[1536,256]{1,0:T(8,128)(2,1)S(1)}, bf16[1536,256]{1,0:T(8,128)(2,1)S(1)}, u32[]{:S(2)}, u32[]{:S(2)}) collective-permute-start(bf16[1536,256]{1,0:T(8,128)(2,1)S(1)} %collective-permute-done.refs_1_), channel_id=1, source_target_pairs={{0,1},{1,2},{2,3},{3,0},{4,5},{5,6},{6,7},{7,4},{8,9},{9,10},{10,1... | collective-permute-start | bytes 2359304 | tf_op jit(solution)/shard_map/ppermute | solution.py:168
  35.0 19.0 %collective-permute-start.5 = (bf16[1536,256]{1,0:T(8,128)(2,1)S(1)}, bf16[1536,256]{1,0:T(8,128)(2,1)S(1)}, u32[]{:S(2)}, u32[]{:S(2)}) collective-permute-start(bf16[1536,256]{1,0:T(8,128)(2,1)S(1)} %collective-permute-done.refs_1_), channel_id=1, source_target_pairs={{0,8},{5,13},{10,2},{15,7},{16,24},{21,29},{26,18},{31,23}} | collective-permute-start | bytes 2359304 | tf_op jit(solution)/shard_map/ppermute | solution.py:24
  38.6 21.6 %collective-permute-start.4 = (bf16[1536,256]{1,0:T(8,128)(2,1)S(1)}, bf16[1536,256]{1,0:T(8,128)(2,1)S(1)}, u32[]{:S(2)}, u32[]{:S(2)}) collective-permute-start(bf16[1536,256]{1,0:T(8,128)(2,1)S(1)} %broadcast_select_fusion.4), channel_id=1, source_target_pairs={{0,4},{8,12},{5,1},{13,9},{2,6},{10,14},{7,3},{15,11},{16,20},{24,... | collective-permute-start | bytes 2359304 | tf_op jit(solution)/shard_map/ppermute | solution.py:24
  40.0 38.0 %collective-permute-start.12 = (bf16[1536,256]{1,0:T(8,128)(2,1)S(1)}, bf16[1536,256]{1,0:T(8,128)(2,1)S(1)}, u32[]{:S(2)}, u32[]{:S(2)}) collective-permute-start(bf16[1536,256]{1,0:T(8,128)(2,1)S(1)} %broadcast_select_fusion), channel_id=1, source_target_pairs={{0,4},{8,12},{5,1},{13,9},{2,6},{10,14},{7,3},{15,11},{16,20},{24,... | collective-permute-start | bytes 2359304 | tf_op jit(solution)/shard_map/ppermute | solution.py:24
  53.9 18.1 %collective-permute-start.2 = (bf16[1536,256]{1,0:T(8,128)(2,1)S(1)}, bf16[1536,256]{1,0:T(8,128)(2,1)S(1)}, u32[]{:S(2)}, u32[]{:S(2)}) collective-permute-start(bf16[1536,256]{1,0:T(8,128)(2,1)S(1)} %collective-permute-done.1.refs_2_), channel_id=1, source_target_pairs={{0,1},{1,2},{2,3},{3,0},{4,5},{5,6},{6,7},{7,4},{8,9},{9,10},{10,1... | collective-permute-start | bytes 2359304 | tf_op jit(solution)/shard_map/ppermute | solution.py:168
  54.0 35.0 %collective-permute-start.6 = (bf16[1536,256]{1,0:T(8,128)(2,1)S(1)}, bf16[1536,256]{1,0:T(8,128)(2,1)S(1)}, u32[]{:S(2)}, u32[]{:S(2)}) collective-permute-start(bf16[1536,256]{1,0:T(8,128)(2,1)S(1)} %broadcast_select_fusion.3), channel_id=1, source_target_pairs={{0,4},{8,12},{5,1},{13,9},{2,6},{10,14},{7,3},{15,11},{16,20},{24,... | collective-permute-start | bytes 2359304 | tf_op jit(solution)/shard_map/ppermute | solution.py:24
  55.4 22.7 %collective-permute-start.7 = (bf16[1536,256]{1,0:T(8,128)(2,1)S(1)}, bf16[1536,256]{1,0:T(8,128)(2,1)S(1)}, u32[]{:S(2)}, u32[]{:S(2)}) collective-permute-start(bf16[1536,256]{1,0:T(8,128)(2,1)S(1)} %collective-permute-done.1.refs_2_), channel_id=1, source_target_pairs={{0,8},{5,13},{10,2},{15,7},{16,24},{21,29},{26,18},{31,23}} | collective-permute-start | bytes 2359304 | tf_op jit(solution)/shard_map/ppermute | solution.py:24
  60.2 30.7 %slice-start = ((s8[4718592]{0:T(1024)(128)(4,1)}), s8[4194304]{0:T(1024)(128)(4,1)S(1)}, s32[]{:S(2)}) async-start(s8[4718592]{0:T(1024)(128)(4,1)} %bitcast.19), calls=%async_computation | async-start | bytes 8388608
  72.0 15.4 %collective-permute-start.9 = (bf16[1536,256]{1,0:T(8,128)(2,1)S(1)}, bf16[1536,256]{1,0:T(8,128)(2,1)S(1)}, u32[]{:S(2)}, u32[]{:S(2)}) collective-permute-start(bf16[1536,256]{1,0:T(8,128)(2,1)S(1)} %collective-permute-done.2.refs_3_), channel_id=1, source_target_pairs={{0,8},{5,13},{10,2},{15,7},{16,24},{21,29},{26,18},{31,23}} | collective-permute-start | bytes 2359304 | tf_op jit(solution)/shard_map/ppermute | solution.py:24
  78.2 12.6 %slice-start.1 = ((s8[4718592]{0:T(1024)(128)(4,1)}), s8[524288]{0:T(1024)(128)(4,1)S(1)}, s32[]{:S(2)}) async-start(s8[4718592]{0:T(1024)(128)(4,1)} %bitcast.19), calls=%async_computation.1 | async-start | bytes 1048576
  78.2 10.9 %collective-permute-start.8 = (bf16[1536,256]{1,0:T(8,128)(2,1)S(1)}, bf16[1536,256]{1,0:T(8,128)(2,1)S(1)}, u32[]{:S(2)}, u32[]{:S(2)}) collective-permute-start(bf16[1536,256]{1,0:T(8,128)(2,1)S(1)} %broadcast_select_fusion.2), channel_id=1, source_target_pairs={{0,4},{8,12},{5,1},{13,9},{2,6},{10,14},{7,3},{15,11},{16,20},{24,... | collective-permute-start | bytes 2359304 | tf_op jit(solution)/shard_map/ppermute | solution.py:24
  87.5 3.2 %collective-permute-start.10 = (bf16[1536,256]{1,0:T(8,128)(2,1)S(1)}, bf16[1536,256]{1,0:T(8,128)(2,1)S(1)}, u32[]{:S(2)}, u32[]{:S(2)}) collective-permute-start(bf16[1536,256]{1,0:T(8,128)(2,1)S(1)} %broadcast_select_fusion.1), channel_id=1, source_target_pairs={{0,4},{8,12},{5,1},{13,9},{2,6},{10,14},{7,3},{15,11},{16,20},{24,... | collective-permute-start | bytes 2359304 | tf_op jit(solution)/shard_map/ppermute | solution.py:24
  98.2 16.2 %collective-permute-start.16 = (bf16[6,384,128]{2,1,0:T(8,128)(2,1)S(1)}, bf16[6,384,128]{2,1,0:T(8,128)(2,1)S(1)}, u32[]{:S(2)}, u32[]{:S(2)}) collective-permute-start(bf16[6,384,128]{2,1,0:T(8,128)(2,1)S(1)} %get-tuple-element.20), channel_id=1, source_target_pairs={{0,16},{16,0},{1,17},{17,1},{2,18},{18,2},{3,19},{19,3},{4,20},{20... | collective-permute-start | bytes 1769480 | tf_op jit(solution)/shard_map/ppermute | solution.py:177
  105.7 21.4 %collective-permute-start.15 = (bf16[6,384,128]{2,1,0:T(8,128)(2,1)S(1)}, bf16[6,384,128]{2,1,0:T(8,128)(2,1)S(1)}, u32[]{:S(2)}, u32[]{:S(2)}) collective-permute-start(bf16[6,384,128]{2,1,0:T(8,128)(2,1)S(1)} %get-tuple-element.18), channel_id=1, source_target_pairs={{0,16},{16,0},{1,17},{17,1},{2,18},{18,2},{3,19},{19,3},{4,20},{20... | collective-permute-start | bytes 1769480 | tf_op jit(solution)/shard_map/ppermute | solution.py:177
  114.6 16.3 %collective-permute-start.17 = (bf16[6,384,128]{2,1,0:T(8,128)(2,1)S(1)}, bf16[6,384,128]{2,1,0:T(8,128)(2,1)S(1)}, u32[]{:S(2)}, u32[]{:S(2)}) collective-permute-start(bf16[6,384,128]{2,1,0:T(8,128)(2,1)S(1)} %add_convert_fusion.3), channel_id=1, source_target_pairs={{0,1},{1,2},{2,3},{3,0},{4,5},{5,6},{6,7},{7,4},{8,9},{9,10},{10,1... | collective-permute-start | bytes 1769480 | tf_op jit(solution)/shard_map/ppermute | solution.py:183
  122.2 16.9 %collective-permute-start.14 = (bf16[6,384,128]{2,1,0:T(8,128)(2,1)S(1)}, bf16[6,384,128]{2,1,0:T(8,128)(2,1)S(1)}, u32[]{:S(2)}, u32[]{:S(2)}) collective-permute-start(bf16[6,384,128]{2,1,0:T(8,128)(2,1)S(1)} %get-tuple-element.16), channel_id=1, source_target_pairs={{0,16},{16,0},{1,17},{17,1},{2,18},{18,2},{3,19},{19,3},{4,20},{20... | collective-permute-start | bytes 1769480 | tf_op jit(solution)/shard_map/ppermute | solution.py:177
  131.1 15.2 %collective-permute-start.18 = (bf16[6,384,128]{2,1,0:T(8,128)(2,1)S(1)}, bf16[6,384,128]{2,1,0:T(8,128)(2,1)S(1)}, u32[]{:S(2)}, u32[]{:S(2)}) collective-permute-start(bf16[6,384,128]{2,1,0:T(8,128)(2,1)S(1)} %add_convert_fusion.2), channel_id=1, source_target_pairs={{0,1},{1,2},{2,3},{3,0},{4,5},{5,6},{6,7},{7,4},{8,9},{9,10},{10,1... | collective-permute-start | bytes 1769480 | tf_op jit(solution)/shard_map/ppermute | solution.py:183
  138.5 13.4 %collective-permute-start.13 = (bf16[6,384,128]{2,1,0:T(8,128)(2,1)S(1)}, bf16[6,384,128]{2,1,0:T(8,128)(2,1)S(1)}, u32[]{:S(2)}, u32[]{:S(2)}) collective-permute-start(bf16[6,384,128]{2,1,0:T(8,128)(2,1)S(1)} %get-tuple-element.14), channel_id=1, source_target_pairs={{0,16},{16,0},{1,17},{17,1},{2,18},{18,2},{3,19},{19,3},{4,20},{20... | collective-permute-start | bytes 1769480 | tf_op jit(solution)/shard_map/ppermute | solution.py:177
  146.4 14.2 %collective-permute-start.19 = (bf16[6,384,128]{2,1,0:T(8,128)(2,1)S(1)}, bf16[6,384,128]{2,1,0:T(8,128)(2,1)S(1)}, u32[]{:S(2)}, u32[]{:S(2)}) collective-permute-start(bf16[6,384,128]{2,1,0:T(8,128)(2,1)S(1)} %add_convert_fusion.1), channel_id=1, source_target_pairs={{0,1},{1,2},{2,3},{3,0},{4,5},{5,6},{6,7},{7,4},{8,9},{9,10},{10,1... | collective-permute-start | bytes 1769480 | tf_op jit(solution)/shard_map/ppermute | solution.py:183
